TPU v7x, 512 devices: a whole 4x8x8 slice. The times are simulated.
512 devices in a mesh: ens: 4 (over y_hi), lat: 8 (over y_lo, x), lon: 16 (over z, core).
Axes of the slice: x: 4, y: 8 (y_hi: 4, y_lo: 2; y = y_hi * 2 + y_lo), z: 8, core: 2. Of those that a mesh axis runs over, the one named last changes fastest.
Arguments:
- initial_state: float32 [24, 128, 2048], P('ens', 'lat', 'lon'), parts along dimension 0, may hold values from -6 to 6
- diffusion: float32 [128, 2048], P('lat', 'lon'), may hold values from 0.05 to 0.2
- mixing: float32 [6, 6], replicated, may hold values from -0.3 to 0.3
- land_mask: int32 [128, 2048], P('lat', 'lon'), may hold values 0 or 1
- first_layer: bfloat16 [128, 54], replicated, may hold values from -0.875 to 0.875
- second_layer: bfloat16 [128, 128], replicated, may hold values from -0.5 to 0.5
- output_layer: bfloat16 [6, 128], replicated, may hold values from -0.5 to 0.5
- cotangent: float32 [24, 128, 2048], P('ens', 'lat', 'lon'), parts along dimension 0, may hold values from -20 to 20
- update_noise: float32 [96256], P('ens'), parts along dimension 0, may hold values from -0.15 to 0.15
Outputs:
- final_state: float32 [24, 128, 2048], P('ens', 'lat', 'lon'), parts along dimension 0
- initial_adjoint: float32 [24, 128, 2048], P('ens', 'lat', 'lon'), parts along dimension 0
- new_params: float32 [96256], P('ens'), parts along dimension 0
- noise_ratio: float32 [4], P('ens'), parts along dimension 0
There are 4 independent parts, one for each index of `ens`. A program takes and returns all parts, laid end to end along the dimension named above; an argument that names none is the same for every part. Nothing has to cross between parts.
All inputs are finite; a program needn't handle non-finite values. No bound on the sum of `land_mask` on one device may be relied on, other than what follows from the above.
Results may differ from a plain program's by a relative error of at most 0.0033.
Values sent between devices are 32-bit elements; how exact they have to be, the bound alone decides.
A program may use at most 64 MiB of HBM per device.

v0:
```python
import jax
import jax.numpy as jnp
from jax import lax
from jax.sharding import PartitionSpec as P

STEPS = 2
closure_dt = 0.1
learn_rate = 0.1
epsilon = 1e-06
offsets = [(row_shift, col_shift) for row_shift in (-1, 0, 1) for col_shift in (-1, 0, 1)]


def with_halo(value, sides, width, wrap):
    for axis, dim in sides:
        devices, length = (lax.axis_size(axis), value.shape[dim])
        up = [(i, (i + 1) % devices) for i in range(devices if wrap else devices - 1)]
        down = [(j, i) for i, j in up]
        last = lax.slice_in_dim(value, length - width, length, axis=dim)
        first = lax.slice_in_dim(value, 0, width, axis=dim)
        before = lax.ppermute(last, axis, up)
        after = lax.ppermute(first, axis, down)
        value = jnp.concatenate([before, value, after], axis=dim)
    return value


def contract_last(left, right):
    return lax.dot_general(
        left, right, (((1,), (1,)), ((), ())), preferred_element_type=jnp.float32
    )


def contract_first(left, right):
    return lax.dot_general(
        left, right, (((0,), (0,)), ((), ())), preferred_element_type=jnp.float32
    )


def build_patch(slab, rows, cols):
    return jnp.concatenate(
        [
            slab[:, 1 + row_shift : 1 + row_shift + rows, 1 + col_shift : 1 + col_shift + cols]
            for row_shift, col_shift in offsets
        ],
        axis=0,
    )


def hidden_layers(flat, first_layer, second_layer):
    hidden_one = jnp.tanh(jnp.dot(first_layer, flat, preferred_element_type=jnp.float32)).astype(
        jnp.bfloat16
    )
    hidden_two = jnp.tanh(
        jnp.dot(second_layer, hidden_one, preferred_element_type=jnp.float32)
    ).astype(jnp.bfloat16)
    return (hidden_one, hidden_two)


def forward_block(slab, mask_rows, diff_rows, mixing, first_layer, second_layer, output_layer):
    fields = slab.shape[0]
    rows = slab.shape[1] - 2
    cols = slab.shape[2] - 2
    count = rows * cols
    patch = build_patch(slab, rows, cols)
    centre = patch[4 * fields : 5 * fields]
    laplace = (
        patch[fields : 2 * fields]
        + patch[3 * fields : 4 * fields]
        + patch[5 * fields : 6 * fields]
        + patch[7 * fields : 8 * fields]
        - 4.0 * centre
    )
    flat = patch.reshape(9 * fields, count).astype(jnp.bfloat16)
    hidden_one, hidden_two = hidden_layers(flat, first_layer, second_layer)
    tendency = jnp.dot(output_layer, hidden_two, preferred_element_type=jnp.float32)
    mixed = jnp.dot(mixing, centre.reshape(fields, count), precision=lax.Precision.HIGHEST)
    update = (
        centre
        + diff_rows[None] * laplace
        + (mixed + closure_dt * tendency).reshape(fields, rows, cols)
    )
    return mask_rows[None] * update


def backward_block(
    slab, adjoint_rows, mask_rows, diff_rows, mixing, first_layer, second_layer, output_layer
):
    fields = slab.shape[0]
    rows = slab.shape[1] - 2
    cols = slab.shape[2] - 2
    count = rows * cols
    patch = build_patch(slab, rows, cols)
    flat = patch.reshape(9 * fields, count).astype(jnp.bfloat16)
    hidden_one, hidden_two = hidden_layers(flat, first_layer, second_layer)
    masked = (mask_rows[None] * adjoint_rows).reshape(fields, count)
    out_grad = (closure_dt * masked).astype(jnp.bfloat16)
    back_two = (
        contract_first(output_layer, out_grad) * (1.0 - jnp.square(hidden_two.astype(jnp.float32)))
    ).astype(jnp.bfloat16)
    back_one = (
        contract_first(second_layer, back_two) * (1.0 - jnp.square(hidden_one.astype(jnp.float32)))
    ).astype(jnp.bfloat16)
    patch_grad = contract_first(first_layer, back_one)
    direct = masked + lax.dot_general(
        mixing,
        masked,
        (((0,), (0,)), ((), ())),
        precision=lax.Precision.HIGHEST,
        preferred_element_type=jnp.float32,
    )
    spread = diff_rows.reshape(1, count) * masked
    blank = jnp.zeros_like(masked)
    extra = jnp.concatenate(
        [blank, spread, blank, spread, direct - 4.0 * spread, spread, blank, spread, blank], axis=0
    )
    patch_grad = (patch_grad + extra).reshape(9 * fields, rows, cols)
    grads = jnp.concatenate(
        [
            contract_last(back_one, flat).ravel(),
            contract_last(back_two, hidden_one).ravel(),
            contract_last(out_grad, hidden_two).ravel(),
        ]
    )
    return (patch_grad, grads)


def on_device(
    initial_state,
    diffusion,
    mixing,
    land_mask,
    first_layer,
    second_layer,
    output_layer,
    cotangent,
    update_noise,
):
    fields, rows, cols = initial_state.shape
    mask = land_mask.astype(jnp.float32)
    state = initial_state
    saved = []
    for step in range(STEPS):
        wide = with_halo(state, (("lon", 2),), 1, True)
        padded = with_halo(wide, (("lat", 1),), 1, False)
        saved.append(padded)
        state = forward_block(
            padded, mask, diffusion, mixing, first_layer, second_layer, output_layer
        )
    adjoint = cotangent
    local_grad = jnp.zeros((first_layer.size + second_layer.size + output_layer.size,), jnp.float32)
    for step in reversed(range(STEPS)):
        patch_grad, grads = backward_block(
            saved[step], adjoint, mask, diffusion, mixing, first_layer, second_layer, output_layer
        )
        local_grad = local_grad + grads
        wide_grad = with_halo(patch_grad, (("lon", 2),), 1, True)
        grad_pad = with_halo(wide_grad, (("lat", 1),), 1, False)
        total = jnp.zeros((fields, rows, cols), jnp.float32)
        for number, (row_shift, col_shift) in enumerate(offsets):
            total = (
                total
                + grad_pad[
                    number * fields : (number + 1) * fields,
                    1 - row_shift : 1 - row_shift + rows,
                    1 - col_shift : 1 - col_shift + cols,
                ]
            )
        adjoint = total
    params_count = local_grad.shape[0]
    band = lax.psum(local_grad, "lon")
    total_grad, band_square = lax.psum((band, jnp.sum(band * band)), "lat")
    grad_square = jnp.sum(total_grad * total_grad)
    noise_ratio = (band_square / (grad_square + epsilon)).reshape(1)
    params = jnp.concatenate(
        [
            first_layer.astype(jnp.float32).ravel(),
            second_layer.astype(jnp.float32).ravel(),
            output_layer.astype(jnp.float32).ravel(),
        ]
    )
    new_params = (
        params
        - learn_rate * total_grad / jnp.sqrt(grad_square / params_count + epsilon)
        + update_noise
    )
    return (state, adjoint, new_params, noise_ratio)


def solution(mesh):
    placed = (
        P("ens", "lat", "lon"),
        P("lat", "lon"),
        P(),
        P("lat", "lon"),
        P(),
        P(),
        P(),
        P("ens", "lat", "lon"),
        P("ens"),
    )
    return jax.shard_map(
        on_device,
        mesh=mesh,
        in_specs=placed,
        out_specs=(P("ens", "lat", "lon"), P("ens", "lat", "lon"), P("ens"), P("ens")),
        check_vma=False,
    )
```

profile of v0, /device:TPU:40, one launch (start us, length us, event | category | flops | bytes accessed | tf_op | source)
XLA Modules:
  0.0 304.6 jit_solution(4147958158141349705)
XLA Ops:
  7.2 1.0 fusion.62
  8.2 8.5 %collective-permute-start.1 = (f32[6,16,1]{2,1,0:T(8,128)S(1)}, f32[6,16,1]{2,1,0:T(8,128)S(1)}, u32[]{:S(2)}, u32[]{:S(2)}) collective-permute-start(f32[6,16,1]{2,1,0:T(8,128)S(1)} %get-tuple-element.31), channel_id=1, source_target_pairs={{1,0},{2,1},{3,2},{4,3},{5,4},{6,5},{7,6},{8,7},{9,8},{10,9},{11,1... | collective-permute-start | bytes 1160 | tf_op jit(solution)/shard_map/ppermute | solution.py:21
  16.7 1.8 collective-permute-done
  18.6 5.5 %collective-permute-start.3 = (f32[6,1,130]{2,1,0:T(1,128)S(1)}, f32[6,1,130]{2,1,0:T(1,128)S(1)}, u32[]{:S(2)}, u32[]{:S(2)}) collective-permute-start(f32[6,1,130]{2,1,0:T(1,128)S(1)} %get-tuple-element.26), channel_id=1, source_target_pairs={{16,0},{32,16},{48,32},{64,48},{80,64},{96,80},{112,96},{17,1},{33... | collective-permute-start | bytes 9368 | tf_op jit(solution)/shard_map/ppermute | solution.py:21
  24.0 1.9 collective-permute-start.2
  26.2 0.5 copy-done.20
  26.7 5.0 %collective-permute-done.2 = f32[6,1,130]{2,1,0:T(1,128)S(1)} collective-permute-done((f32[6,1,130]{2,1,0:T(1,128)S(1)}, f32[6,1,130]{2,1,0:T(1,128)S(1)}, u32[]{:S(2)}, u32[]{:S(2)}) %collective-permute-start.2) | collective-permute-done | bytes 3152 | tf_op jit(solution)/shard_map/ppermute | solution.py:20
  32.5 0.6 copy-done.9
  33.2 0.4 fusion
  33.6 0.4 copy-done.6
  33.9 0.3 fusion.1
  34.2 0.4 copy-done.19
  34.6 0.2 fusion.17
  34.9 0.5 copy-done.11
  35.5 3.0 collective-permute-start.5
  38.6 0.8 reshape.86
  39.4 0.9 collective-permute-done.4
  40.4 1.9 collective-permute-start.7
  42.3 3.9 %collective-permute-start.6 = (f32[6,1,130]{2,1,0:T(1,128)S(1)}, f32[6,1,130]{2,1,0:T(1,128)S(1)}, u32[]{:S(2)}, u32[]{:S(2)}) collective-permute-start(f32[6,1,130]{2,1,0:T(1,128)S(1)} %get-tuple-element.23), channel_id=1, source_target_pairs={{0,16},{16,32},{32,48},{48,64},{64,80},{80,96},{96,112},{1,17},{17... | collective-permute-start | bytes 9368 | tf_op jit(solution)/shard_map/ppermute | solution.py:20
  46.2 0.2 fusion.25
  46.5 3.5 %collective-permute-done.6 = f32[6,1,130]{2,1,0:T(1,128)S(1)} collective-permute-done((f32[6,1,130]{2,1,0:T(1,128)S(1)}, f32[6,1,130]{2,1,0:T(1,128)S(1)}, u32[]{:S(2)}, u32[]{:S(2)}) %collective-permute-start.6) | collective-permute-done | bytes 3152 | tf_op jit(solution)/shard_map/ppermute | solution.py:20
  50.8 0.4 fusion.2
  51.2 0.3 fusion.3
  51.5 0.2 fusion.18
  51.8 0.6 copy-done.18
  52.3 0.8 multiply_bitcast_fusion
  53.1 0.4 fusion.4
  53.5 0.9 fusion.13
  54.4 0.7 copy-done.7
  55.1 0.3 fusion.5
  55.4 1.0 fusion.63
  56.4 11.9 %concatenate.120 = f32[54,2048]{1,0:T(8,128)} concatenate(f32[6,2048]{1,0:T(8,128)S(1)} %broadcast.26, f32[6,2048]{1,0:T(8,128)S(1)} %bitcast_multiply_fusion.2, f32[6,2048]{1,0:T(8,128)S(1)} %broadcast.26, f32[6,2048]{1,0:T(8,128)S(1)} %bitcast_multiply_fusion.2, f32[6,2048]{1,0:T(8,128)} %fusion.13, f32[6,2048]{1,0:T(8,128)S(1)} %bitcast_multiply_fusion.2, ...), dimensions={0} | concatenate | bytes 884736 | tf_op jit(solution)/shard_map/concatenate | solution.py:112
  68.3 1.5 fusion.9
  69.8 0.2 fusion.60
  70.0 2.9 collective-permute-start.9
  73.0 1.0 convolution_bitcast_fusion.3
  74.0 5.0 %collective-permute-done.8 = f32[54,16,1]{2,1,0:T(8,128)S(1)} collective-permute-done((f32[54,16,1]{2,1,0:T(8,128)S(1)}, f32[54,16,1]{2,1,0:T(8,128)S(1)}, u32[]{:S(2)}, u32[]{:S(2)}) %collective-permute-start.8) | collective-permute-done | bytes 3488 | tf_op jit(solution)/shard_map/ppermute | solution.py:20
  79.0 1.0 pad_maximum_fusion.7
  80.0 2.0 collective-permute-start.10
  82.1 4.1 %collective-permute-start.11 = (f32[54,1,130]{2,1,0:T(1,128)}, f32[54,1,130]{2,1,0:T(1,128)}, u32[]{:S(2)}, u32[]{:S(2)}) collective-permute-start(f32[54,1,130]{2,1,0:T(1,128)} %get-tuple-element.15), channel_id=1, source_target_pairs={{0,16},{16,32},{32,48},{48,64},{64,80},{80,96},{96,112},{1,17},{17... | collective-permute-start | bytes 84248 | tf_op jit(solution)/shard_map/ppermute | solution.py:20
  86.5 4.2 %collective-permute-done.11 = f32[54,1,130]{2,1,0:T(1,128)} collective-permute-done((f32[54,1,130]{2,1,0:T(1,128)}, f32[54,1,130]{2,1,0:T(1,128)}, u32[]{:S(2)}, u32[]{:S(2)}) %collective-permute-start.11) | collective-permute-done | bytes 28112 | tf_op jit(solution)/shard_map/ppermute | solution.py:20
  90.7 1.0 fusion.40
  91.9 0.4 fusion.6
  92.3 0.3 convolution_bitcast_fusion.2
  92.6 0.3 fusion.7
  92.9 0.3 fusion.11
  93.2 0.3 fusion.64
  93.7 0.6 concatenate.126
  94.4 0.4 fusion.8
  94.9 0.2 fusion.59
  95.1 2.9 collective-permute-start.13
  98.1 0.7 maximum_add_fusion
  98.8 5.3 %collective-permute-done.12 = f32[54,16,1]{2,1,0:T(8,128)S(1)} collective-permute-done((f32[54,16,1]{2,1,0:T(8,128)S(1)}, f32[54,16,1]{2,1,0:T(8,128)S(1)}, u32[]{:S(2)}, u32[]{:S(2)}) %collective-permute-start.12) | collective-permute-done | bytes 3488 | tf_op jit(solution)/shard_map/ppermute | solution.py:20
  104.1 0.4 pad_maximum_fusion.4
  104.5 1.9 collective-permute-start.14
  106.4 3.9 %collective-permute-start.15 = (f32[54,1,130]{2,1,0:T(1,128)S(1)}, f32[54,1,130]{2,1,0:T(1,128)S(1)}, u32[]{:S(2)}, u32[]{:S(2)}) collective-permute-start(f32[54,1,130]{2,1,0:T(1,128)S(1)} %get-tuple-element.13), channel_id=1, source_target_pairs={{0,16},{16,32},{32,48},{48,64},{64,80},{80,96},{96,112},{1,17},{17... | collective-permute-start | bytes 84248 | tf_op jit(solution)/shard_map/ppermute | solution.py:20
  110.3 93.3 %all-reduce.3.cloned.1.call-done = f32[24064]{0:T(1024)} async-done(((f32[24064]{0:T(1024)}), f32[24064]{0:T(1024)}) %all-reduce.3.cloned.1.call-update) | async-done | bytes 96272 | tf_op jit(solution)/shard_map/psum | solution.py:169
  203.6 1.5 multiply_reduce_fusion
  205.1 0.7 all-reduce.5.cloned.1.call-update
  205.9 0.9 fusion.34
  206.8 20.1 %psum.23 = f32[]{:T(128)} all-reduce(f32[]{:T(128)} %multiply_reduce_fusion), channel_id=1, replica_groups=mesh['ens'=4,'lat'=8,'lon'=16] {'lat'}, use_global_device_ids=true, to_apply=%region_4.0 | all-reduce | flops 1 | bytes 8 | tf_op jit(solution)/shard_map/psum | solution.py:170
  226.9 64.6 %all-reduce.5.cloned.1.call-done = f32[24064]{0:T(1024)} async-done(((f32[24064]{0:T(1024)}), f32[24064]{0:T(1024)}) %all-reduce.5.cloned.1.call-update) | async-done | bytes 96272 | tf_op jit(solution)/shard_map/psum | solution.py:170
  291.5 1.5 multiply_reduce_fusion.1
  295.1 1.6 subtract_add_fusion
  (95 shorter events, 3.6 us)
Async XLA Ops:
  7.2 18.8 %copy-start = (f32[6,6]{1,0:T(8,128)S(1)}, f32[6,6]{1,0:T(8,128)}, u32[]{:S(2)}) copy-start(f32[6,6]{1,0:T(8,128)} %param.11) | copy-start | bytes 436
  7.2 11.3 %copy-start.1 = (f32[6,16,128]{2,1,0:T(8,128)S(1)}, f32[6,16,128]{2,1,0:T(8,128)}, u32[]{:S(2)}) copy-start(f32[6,16,128]{2,1,0:T(8,128)} %param.9) | copy-start | bytes 147460
  7.2 196.4 %all-reduce.3.cloned.1.call-start = ((), (), s32[]{:S(2)}) async-start(), calls=%async_computation | async-start | bytes 196608 | tf_op jit(solution)/shard_map/psum | solution.py:169
  8.2 10.3 %collective-permute-start = (f32[6,16,1]{2,1,0:T(8,128)S(1)}, f32[6,16,1]{2,1,0:T(8,128)S(1)}, u32[]{:S(2)}, u32[]{:S(2)}) collective-permute-start(f32[6,16,1]{2,1,0:T(8,128)S(1)} %get-tuple-element.30), channel_id=1, source_target_pairs={{0,1},{1,2},{2,3},{3,4},{4,5},{5,6},{6,7},{7,8},{8,9},{9,10},{10,1... | collective-permute-start | bytes 1160 | tf_op jit(solution)/shard_map/ppermute | solution.py:20
  8.2 10.2 %collective-permute-start.1 = (f32[6,16,1]{2,1,0:T(8,128)S(1)}, f32[6,16,1]{2,1,0:T(8,128)S(1)}, u32[]{:S(2)}, u32[]{:S(2)}) collective-permute-start(f32[6,16,1]{2,1,0:T(8,128)S(1)} %get-tuple-element.31), channel_id=1, source_target_pairs={{1,0},{2,1},{3,2},{4,3},{5,4},{6,5},{7,6},{8,7},{9,8},{10,9},{11,1... | collective-permute-start | bytes 1160 | tf_op jit(solution)/shard_map/ppermute | solution.py:21
  18.6 8.1 %collective-permute-start.3 = (f32[6,1,130]{2,1,0:T(1,128)S(1)}, f32[6,1,130]{2,1,0:T(1,128)S(1)}, u32[]{:S(2)}, u32[]{:S(2)}) collective-permute-start(f32[6,1,130]{2,1,0:T(1,128)S(1)} %get-tuple-element.26), channel_id=1, source_target_pairs={{16,0},{32,16},{48,32},{64,48},{80,64},{96,80},{112,96},{17,1},{33... | collective-permute-start | bytes 9368 | tf_op jit(solution)/shard_map/ppermute | solution.py:21
  24.0 7.6 %collective-permute-start.2 = (f32[6,1,130]{2,1,0:T(1,128)S(1)}, f32[6,1,130]{2,1,0:T(1,128)S(1)}, u32[]{:S(2)}, u32[]{:S(2)}) collective-permute-start(f32[6,1,130]{2,1,0:T(1,128)S(1)} %get-tuple-element.27), channel_id=1, source_target_pairs={{0,16},{16,32},{32,48},{48,64},{64,80},{80,96},{96,112},{1,17},{17... | collective-permute-start | bytes 9368 | tf_op jit(solution)/shard_map/ppermute | solution.py:20
  26.0 0.7 copy-start.20
  26.7 25.1 %copy-start.14 = (f32[16,128]{1,0:T(8,128)}, f32[16,128]{1,0:T(8,128)S(1)}, u32[]{:S(2)}) copy-start(f32[16,128]{1,0:T(8,128)S(1)} %convert_element_type.70) | copy-start | bytes 24580
  32.5 0.7 copy-start.9
  33.2 0.8 copy-start.6
  33.9 0.7 copy-start.19
  34.6 0.7 copy-start.11
  35.5 4.7 %collective-permute-start.4 = (f32[6,16,1]{2,1,0:T(8,128)S(1)}, f32[6,16,1]{2,1,0:T(8,128)S(1)}, u32[]{:S(2)}, u32[]{:S(2)}) collective-permute-start(f32[6,16,1]{2,1,0:T(8,128)S(1)} %get-tuple-element.28), channel_id=1, source_target_pairs={{0,1},{1,2},{2,3},{3,4},{4,5},{5,6},{6,7},{7,8},{8,9},{9,10},{10,1... | collective-permute-start | bytes 1160 | tf_op jit(solution)/shard_map/ppermute | solution.py:20
  35.5 4.7 %collective-permute-start.5 = (f32[6,16,1]{2,1,0:T(8,128)S(1)}, f32[6,16,1]{2,1,0:T(8,128)S(1)}, u32[]{:S(2)}, u32[]{:S(2)}) collective-permute-start(f32[6,16,1]{2,1,0:T(8,128)S(1)} %get-tuple-element.29), channel_id=1, source_target_pairs={{1,0},{2,1},{3,2},{4,3},{5,4},{6,5},{7,6},{8,7},{9,8},{10,9},{11,1... | collective-permute-start | bytes 1160 | tf_op jit(solution)/shard_map/ppermute | solution.py:21
  40.4 6.1 %collective-permute-start.7 = (f32[6,1,130]{2,1,0:T(1,128)S(1)}, f32[6,1,130]{2,1,0:T(1,128)S(1)}, u32[]{:S(2)}, u32[]{:S(2)}) collective-permute-start(f32[6,1,130]{2,1,0:T(1,128)S(1)} %get-tuple-element.22), channel_id=1, source_target_pairs={{16,0},{32,16},{48,32},{64,48},{80,64},{96,80},{112,96},{17,1},{33... | collective-permute-start | bytes 9368 | tf_op jit(solution)/shard_map/ppermute | solution.py:21
  42.3 7.6 %collective-permute-start.6 = (f32[6,1,130]{2,1,0:T(1,128)S(1)}, f32[6,1,130]{2,1,0:T(1,128)S(1)}, u32[]{:S(2)}, u32[]{:S(2)}) collective-permute-start(f32[6,1,130]{2,1,0:T(1,128)S(1)} %get-tuple-element.23), channel_id=1, source_target_pairs={{0,16},{16,32},{32,48},{48,64},{64,80},{80,96},{96,112},{1,17},{17... | collective-permute-start | bytes 9368 | tf_op jit(solution)/shard_map/ppermute | solution.py:20
  51.5 0.8 copy-start.18
  53.1 1.3 copy-start.4
  54.3 0.8 copy-start.7
  70.0 8.9 %collective-permute-start.8 = (f32[54,16,1]{2,1,0:T(8,128)S(1)}, f32[54,16,1]{2,1,0:T(8,128)S(1)}, u32[]{:S(2)}, u32[]{:S(2)}) collective-permute-start(f32[54,16,1]{2,1,0:T(8,128)S(1)} %get-tuple-element.18), channel_id=1, source_target_pairs={{0,1},{1,2},{2,3},{3,4},{4,5},{5,6},{6,7},{7,8},{8,9},{9,10},{10,1... | collective-permute-start | bytes 10376 | tf_op jit(solution)/shard_map/ppermute | solution.py:20
  70.0 8.9 %collective-permute-start.9 = (f32[54,16,1]{2,1,0:T(8,128)S(1)}, f32[54,16,1]{2,1,0:T(8,128)S(1)}, u32[]{:S(2)}, u32[]{:S(2)}) collective-permute-start(f32[54,16,1]{2,1,0:T(8,128)S(1)} %get-tuple-element.19), channel_id=1, source_target_pairs={{1,0},{2,1},{3,2},{4,3},{5,4},{6,5},{7,6},{8,7},{9,8},{10,9},{11,1... | collective-permute-start | bytes 10376 | tf_op jit(solution)/shard_map/ppermute | solution.py:21
  74.0 12.2 %copy-start.5 = (f32[1,6,16,128]{3,2,1,0:T(8,128)S(1)}, f32[1,6,16,128]{3,2,1,0:T(8,128)}, u32[]{:S(2)}) copy-start(f32[1,6,16,128]{3,2,1,0:T(8,128)} %copy-done.4) | copy-start | bytes 147460
  79.0 1.1 copy-start.2
  80.0 10.7 %copy-start.3 = (f32[54,16,1]{2,1,0:T(8,128)S(1)}, f32[54,16,1]{2,1,0:T(8,128)}, u32[]{:S(2)}) copy-start(f32[54,16,1]{2,1,0:T(8,128)} %copy-done.2) | copy-start | bytes 10372
  80.0 6.5 %collective-permute-start.10 = (f32[54,1,130]{2,1,0:T(1,128)}, f32[54,1,130]{2,1,0:T(1,128)S(1)}, u32[]{:S(2)}, u32[]{:S(2)}) collective-permute-start(f32[54,1,130]{2,1,0:T(1,128)} %get-tuple-element.14), channel_id=1, source_target_pairs={{16,0},{32,16},{48,32},{64,48},{80,64},{96,80},{112,96},{17,1},{33... | collective-permute-start | bytes 84248 | tf_op jit(solution)/shard_map/ppermute | solution.py:21
  82.1 4.3 %copy-start.12 = (f32[128,54]{1,0:T(8,128)S(1)}, f32[128,54]{1,0:T(8,128)}, u32[]{:S(2)}) copy-start(f32[128,54]{1,0:T(8,128)} %fusion.63) | copy-start | bytes 82948
  82.1 8.6 %collective-permute-start.11 = (f32[54,1,130]{2,1,0:T(1,128)}, f32[54,1,130]{2,1,0:T(1,128)}, u32[]{:S(2)}, u32[]{:S(2)}) collective-permute-start(f32[54,1,130]{2,1,0:T(1,128)} %get-tuple-element.15), channel_id=1, source_target_pairs={{0,16},{16,32},{32,48},{48,64},{64,80},{80,96},{96,112},{1,17},{17... | collective-permute-start | bytes 84248 | tf_op jit(solution)/shard_map/ppermute | solution.py:20
  86.3 4.4 %copy-start.15 = (f32[16,128]{1,0:T(8,128)S(1)}, f32[16,128]{1,0:T(8,128)}, u32[]{:S(2)}) copy-start(f32[16,128]{1,0:T(8,128)} %copy-done.14) | copy-start | bytes 24580
  93.7 0.7 copy-start.10
  94.9 3.2 %copy-start.13 = (f32[16384]{0:T(1024)S(1)}, f32[16384]{0:T(1024)}, u32[]{:S(2)}) copy-start(f32[16384]{0:T(1024)} %convolution_bitcast_fusion.3) | copy-start | bytes 196612
  95.1 8.9 %collective-permute-start.12 = (f32[54,16,1]{2,1,0:T(8,128)S(1)}, f32[54,16,1]{2,1,0:T(8,128)S(1)}, u32[]{:S(2)}, u32[]{:S(2)}) collective-permute-start(f32[54,16,1]{2,1,0:T(8,128)S(1)} %get-tuple-element.16), channel_id=1, source_target_pairs={{0,1},{1,2},{2,3},{3,4},{4,5},{5,6},{6,7},{7,8},{8,9},{9,10},{10,1... | collective-permute-start | bytes 10376 | tf_op jit(solution)/shard_map/ppermute | solution.py:20
  95.1 8.9 %collective-permute-start.13 = (f32[54,16,1]{2,1,0:T(8,128)S(1)}, f32[54,16,1]{2,1,0:T(8,128)S(1)}, u32[]{:S(2)}, u32[]{:S(2)}) collective-permute-start(f32[54,16,1]{2,1,0:T(8,128)S(1)} %get-tuple-element.17), channel_id=1, source_target_pairs={{1,0},{2,1},{3,2},{4,3},{5,4},{6,5},{7,6},{8,7},{9,8},{10,9},{11,1... | collective-permute-start | bytes 10376 | tf_op jit(solution)/shard_map/ppermute | solution.py:21
  104.5 101.4 %collective-permute-start.14 = (f32[54,1,130]{2,1,0:T(1,128)S(1)}, f32[54,1,130]{2,1,0:T(1,128)S(1)}, u32[]{:S(2)}, u32[]{:S(2)}) collective-permute-start(f32[54,1,130]{2,1,0:T(1,128)S(1)} %get-tuple-element.12), channel_id=1, source_target_pairs={{16,0},{32,16},{48,32},{64,48},{80,64},{96,80},{112,96},{17,1},{33... | collective-permute-start | bytes 84248 | tf_op jit(solution)/shard_map/ppermute | solution.py:21
  106.4 99.5 %collective-permute-start.15 = (f32[54,1,130]{2,1,0:T(1,128)S(1)}, f32[54,1,130]{2,1,0:T(1,128)S(1)}, u32[]{:S(2)}, u32[]{:S(2)}) collective-permute-start(f32[54,1,130]{2,1,0:T(1,128)S(1)} %get-tuple-element.13), channel_id=1, source_target_pairs={{0,16},{16,32},{32,48},{48,64},{64,80},{80,96},{96,112},{1,17},{17... | collective-permute-start | bytes 84248 | tf_op jit(solution)/shard_map/ppermute | solution.py:20
  205.1 86.4 %all-reduce.5.cloned.1.call-start = ((), (), s32[]{:S(2)}) async-start(), calls=%async_computation.1 | async-start | bytes 196608 | tf_op jit(solution)/shard_map/psum | solution.py:170
  205.9 89.2 %copy-start.16 = (f32[24064]{0:T(1024)S(1)}, f32[24064]{0:T(1024)}, u32[]{:S(2)}) copy-start(f32[24064]{0:T(1024)} %param.17) | copy-start | bytes 288772
  226.9 68.2 %copy-start.8 = (bf16[128,128]{1,0:T(8,128)(2,1)S(1)}, bf16[128,128]{1,0:T(8,128)(2,1)}, u32[]{:S(2)}) copy-start(bf16[128,128]{1,0:T(8,128)(2,1)} %param.14) | copy-start | bytes 98308
  291.5 3.6 %copy-start.17 = (bf16[6912]{0:T(1024)(128)(2,1)S(1)}, bf16[6912]{0:T(1024)(128)(2,1)}, u32[]{:S(2)}) copy-start(bf16[6912]{0:T(1024)(128)(2,1)} %reshape.86) | copy-start | bytes 41476
Sparse Core Ops, SparseCore 0:
  98.9 104.6 all-reduce.2
  209.1 82.3 all-reduce.4
where the time goes:
time: 306 us; the launch traced here: 305 us
  waiting for transfers between devices  184 us (60%)
  starting transfers between devices  42.6 us (14%)
  local copies, waits for them, and re-layouts  20.1 us (7%)
  blocking collectives  20.1 us (7%)
  between operations  17.7 us (6%)
  other arithmetic  10.5 us (3%)
  matrix products  9.52 us (3%)
    psum x1, waiting for transfers between devices, on_device(): band = lax.psum(local_grad, 'lon')  93.3 us
    psum x1, waiting for transfers between devices, on_device(): total_grad, band_square = lax.psum((band, jnp.sum(band * band)), 'lat')  64.6 us
    ppermute x8, starting transfers between devices, with_halo(): after = lax.ppermute(first, axis, down)  28.7 us
    ppermute x8, waiting for transfers between devices, with_halo(): before = lax.ppermute(last, axis, up)  25.5 us
    psum x1, blocking collectives, on_device(): total_grad, band_square = lax.psum((band, jnp.sum(band * band)), 'lat')  20.1 us
    ppermute x8, starting transfers between devices, with_halo(): before = lax.ppermute(last, axis, up)  13.9 us
    concatenate x2, local copies, waits for them, and re-layouts, backward_block(): jnp.concatenate([blank, spread, blank, spread, direct - 4.0 * spread, spr...  12.4 us
  transfers between devices with their start and end apart: 18, of which 9 were waited for; matrix products, arithmetic and copies ran while one was open for 2% of the time, Pallas kernels for 0%

commit v1 on v0

--- a/solution.py
+++ b/solution.py
@@ -166,7 +166,7 @@
             )
         adjoint = total
     params_count = local_grad.shape[0]
-    band = lax.psum(local_grad, "lon")
+    band = jnp.sum(lax.all_gather(local_grad, "lon"), axis=0)
     total_grad, band_square = lax.psum((band, jnp.sum(band * band)), "lat")
     grad_square = jnp.sum(total_grad * total_grad)
     noise_ratio = (band_square / (grad_square + epsilon)).reshape(1)

time: 306 us -> 222 us (0.73)
  waiting for transfers between devices: 184 us -> 112 us
  local copies, waits for them, and re-layouts: 20.1 us -> 4.39 us
  other arithmetic: 10.5 us -> 16.8 us
    psum x1 -> x0, waiting for transfers between devices: 93.3 us -> none  [on_device(): band = lax.psum(local_grad, 'lon')]
    all_gather x0 -> x1, waiting for transfers between devices: none -> 20 us  [on_device(): band = jnp.sum(lax.all_gather(local_grad, 'lon'), axis=0)]
    concatenate x2, local copies, waits for them, and re-layouts: 12.4 us -> 1.13 us  [backward_block(): jnp.concatenate([blank, spread, blank, spread, direct - 4.0 * spread, spr...]
    unnamed x61 -> x37, local copies, waits for them, and re-layouts: 4.9 us -> 1.1 us
    unnamed x8 -> x9, other arithmetic: 2.13 us -> 5.38 us
  transfers between devices with their start and end apart: 18 -> 18, of which waited for: 9 -> 11; matrix products, arithmetic and copies ran while one was open for 2% -> 4% of each run, Pallas kernels for 0% -> 0%
where the time goes in v1:
time: 222 us; the launch traced here: 221 us
  waiting for transfers between devices  112 us (50%)
  starting transfers between devices  42.4 us (19%)
  blocking collectives  20.2 us (9%)
  between operations  17.7 us (8%)
  other arithmetic  16.8 us (8%)
  matrix products  7.42 us (3%)
  local copies, waits for them, and re-layouts  4.39 us (2%)
    psum x1, waiting for transfers between devices, on_device(): total_grad, band_square = lax.psum((band, jnp.sum(band * band)), 'lat')  63 us
    ppermute x8, starting transfers between devices, with_halo(): after = lax.ppermute(first, axis, down)  28.7 us
    ppermute x8, waiting for transfers between devices, with_halo(): before = lax.ppermute(last, axis, up)  27.1 us
    psum x1, blocking collectives, on_device(): total_grad, band_square = lax.psum((band, jnp.sum(band * band)), 'lat')  20.2 us
    all_gather x1, waiting for transfers between devices, on_device(): band = jnp.sum(lax.all_gather(local_grad, 'lon'), axis=0)  20 us
    ppermute x8, starting transfers between devices, with_halo(): before = lax.ppermute(last, axis, up)  13.7 us
    unnamed x9, other arithmetic  5.38 us
  transfers between devices with their start and end apart: 18, of which 11 were waited for; matrix products, arithmetic and copies ran while one was open for 4% of the time, Pallas kernels for 0%

profile of v1, /device:TPU:40, one launch (start us, length us, event | category | flops | bytes accessed | tf_op | source)
XLA Modules:
  0.0 220.8 jit_solution(1539568956006518721)
XLA Ops:
  7.2 1.0 fusion.63
  8.2 8.5 %collective-permute-start.1 = (f32[6,16,1]{2,1,0:T(8,128)S(1)}, f32[6,16,1]{2,1,0:T(8,128)S(1)}, u32[]{:S(2)}, u32[]{:S(2)}) collective-permute-start(f32[6,16,1]{2,1,0:T(8,128)S(1)} %get-tuple-element.31), channel_id=1, source_target_pairs={{1,0},{2,1},{3,2},{4,3},{5,4},{6,5},{7,6},{8,7},{9,8},{10,9},{11,1... | collective-permute-start | bytes 1160 | tf_op jit(solution)/shard_map/ppermute | solution.py:21
  16.7 1.8 collective-permute-done
  18.4 0.9 pad_maximum_fusion.31
  19.3 5.5 %collective-permute-start.3 = (f32[6,1,130]{2,1,0:T(1,128)S(1)}, f32[6,1,130]{2,1,0:T(1,128)S(1)}, u32[]{:S(2)}, u32[]{:S(2)}) collective-permute-start(f32[6,1,130]{2,1,0:T(1,128)S(1)} %get-tuple-element.26), channel_id=1, source_target_pairs={{16,0},{32,16},{48,32},{64,48},{80,64},{96,80},{112,96},{17,1},{33... | collective-permute-start | bytes 9368 | tf_op jit(solution)/shard_map/ppermute | solution.py:21
  24.8 1.9 collective-permute-start.2
  26.7 1.0 fusion.29
  27.7 0.7 convert_element_type.70
  28.4 4.0 %collective-permute-done.2 = f32[6,1,130]{2,1,0:T(1,128)S(1)} collective-permute-done((f32[6,1,130]{2,1,0:T(1,128)S(1)}, f32[6,1,130]{2,1,0:T(1,128)S(1)}, u32[]{:S(2)}, u32[]{:S(2)}) %collective-permute-start.2) | collective-permute-done | bytes 3152 | tf_op jit(solution)/shard_map/ppermute | solution.py:20
  32.4 1.0 fusion.58
  33.6 0.9 constant_dynamic-update-slice_fusion.5
  34.5 0.8 constant_dynamic-update-slice_fusion.4
  35.4 0.9 constant_dynamic-update-slice_fusion.3
  36.6 0.4 fusion
  37.0 0.3 fusion.1
  37.3 0.2 fusion.17
  37.8 3.0 %collective-permute-start.5 = (f32[6,16,1]{2,1,0:T(8,128)S(1)}, f32[6,16,1]{2,1,0:T(8,128)S(1)}, u32[]{:S(2)}, u32[]{:S(2)}) collective-permute-start(f32[6,16,1]{2,1,0:T(8,128)S(1)} %get-tuple-element.29), channel_id=1, source_target_pairs={{1,0},{2,1},{3,2},{4,3},{5,4},{6,5},{7,6},{8,7},{9,8},{10,9},{11,1... | collective-permute-start | bytes 1160 | tf_op jit(solution)/shard_map/ppermute | solution.py:21
  40.7 1.8 collective-permute-done.4
  42.6 2.0 collective-permute-start.7
  44.7 3.8 %collective-permute-start.6 = (f32[6,1,130]{2,1,0:T(1,128)S(1)}, f32[6,1,130]{2,1,0:T(1,128)S(1)}, u32[]{:S(2)}, u32[]{:S(2)}) collective-permute-start(f32[6,1,130]{2,1,0:T(1,128)S(1)} %get-tuple-element.23), channel_id=1, source_target_pairs={{0,16},{16,32},{32,48},{48,64},{64,80},{80,96},{96,112},{1,17},{17... | collective-permute-start | bytes 9368 | tf_op jit(solution)/shard_map/ppermute | solution.py:20
  48.7 3.6 %collective-permute-done.6 = f32[6,1,130]{2,1,0:T(1,128)S(1)} collective-permute-done((f32[6,1,130]{2,1,0:T(1,128)S(1)}, f32[6,1,130]{2,1,0:T(1,128)S(1)}, u32[]{:S(2)}, u32[]{:S(2)}) %collective-permute-start.6) | collective-permute-done | bytes 3152 | tf_op jit(solution)/shard_map/ppermute | solution.py:20
  53.2 0.4 fusion.2
  53.6 0.3 fusion.3
  53.9 0.2 fusion.18
  54.1 0.8 multiply_bitcast_fusion
  54.9 0.4 fusion.4
  55.3 0.3 fusion.65
  55.6 0.3 fusion.5
  55.9 0.3 fusion.13
  56.2 0.3 fusion.64
  56.6 0.6 concatenate.146
  57.1 0.4 fusion.9
  57.7 0.2 fusion.61
  57.9 2.9 %collective-permute-start.9 = (f32[54,16,1]{2,1,0:T(8,128)S(1)}, f32[54,16,1]{2,1,0:T(8,128)S(1)}, u32[]{:S(2)}, u32[]{:S(2)}) collective-permute-start(f32[54,16,1]{2,1,0:T(8,128)S(1)} %get-tuple-element.19), channel_id=1, source_target_pairs={{1,0},{2,1},{3,2},{4,3},{5,4},{6,5},{7,6},{8,7},{9,8},{10,9},{11,1... | collective-permute-start | bytes 10376 | tf_op jit(solution)/shard_map/ppermute | solution.py:21
  60.9 5.9 %collective-permute-done.8 = f32[54,16,1]{2,1,0:T(8,128)S(1)} collective-permute-done((f32[54,16,1]{2,1,0:T(8,128)S(1)}, f32[54,16,1]{2,1,0:T(8,128)S(1)}, u32[]{:S(2)}, u32[]{:S(2)}) %collective-permute-start.8) | collective-permute-done | bytes 3488 | tf_op jit(solution)/shard_map/ppermute | solution.py:20
  66.8 1.0 pad_maximum_fusion.7
  67.9 1.9 collective-permute-start.10
  69.8 3.9 %collective-permute-start.11 = (f32[54,1,130]{2,1,0:T(1,128)}, f32[54,1,130]{2,1,0:T(1,128)}, u32[]{:S(2)}, u32[]{:S(2)}) collective-permute-start(f32[54,1,130]{2,1,0:T(1,128)} %get-tuple-element.15), channel_id=1, source_target_pairs={{0,16},{16,32},{32,48},{48,64},{64,80},{80,96},{96,112},{1,17},{17... | collective-permute-start | bytes 84248 | tf_op jit(solution)/shard_map/ppermute | solution.py:20
  74.2 4.0 %collective-permute-done.11 = f32[54,1,130]{2,1,0:T(1,128)} collective-permute-done((f32[54,1,130]{2,1,0:T(1,128)}, f32[54,1,130]{2,1,0:T(1,128)}, u32[]{:S(2)}, u32[]{:S(2)}) %collective-permute-start.11) | collective-permute-done | bytes 28112 | tf_op jit(solution)/shard_map/ppermute | solution.py:20
  78.3 1.0 fusion.41
  79.5 0.4 fusion.6
  79.9 0.3 fusion.67
  80.2 0.3 fusion.7
  80.5 0.3 fusion.66
  81.0 0.8 fusion.19
  82.1 0.3 fusion.11
  82.4 0.6 concatenate.152
  83.0 0.4 fusion.8
  83.5 0.2 fusion.60
  83.7 2.9 %collective-permute-start.13 = (f32[54,16,1]{2,1,0:T(8,128)S(1)}, f32[54,16,1]{2,1,0:T(8,128)S(1)}, u32[]{:S(2)}, u32[]{:S(2)}) collective-permute-start(f32[54,16,1]{2,1,0:T(8,128)S(1)} %get-tuple-element.17), channel_id=1, source_target_pairs={{1,0},{2,1},{3,2},{4,3},{5,4},{6,5},{7,6},{8,7},{9,8},{10,9},{11,1... | collective-permute-start | bytes 10376 | tf_op jit(solution)/shard_map/ppermute | solution.py:21
  86.7 5.9 %collective-permute-done.12 = f32[54,16,1]{2,1,0:T(8,128)S(1)} collective-permute-done((f32[54,16,1]{2,1,0:T(8,128)S(1)}, f32[54,16,1]{2,1,0:T(8,128)S(1)}, u32[]{:S(2)}, u32[]{:S(2)}) %collective-permute-start.12) | collective-permute-done | bytes 3488 | tf_op jit(solution)/shard_map/ppermute | solution.py:20
  92.7 0.9 collective-permute-done.13
  93.5 0.4 pad_maximum_fusion.4
  93.9 1.9 collective-permute-start.14
  95.9 4.1 %collective-permute-start.15 = (f32[54,1,130]{2,1,0:T(1,128)S(1)}, f32[54,1,130]{2,1,0:T(1,128)S(1)}, u32[]{:S(2)}, u32[]{:S(2)}) collective-permute-start(f32[54,1,130]{2,1,0:T(1,128)S(1)} %get-tuple-element.13), channel_id=1, source_target_pairs={{0,16},{16,32},{32,48},{48,64},{64,80},{80,96},{96,112},{1,17},{17... | collective-permute-start | bytes 84248 | tf_op jit(solution)/shard_map/ppermute | solution.py:20
  100.0 20.0 %all-gather.3.cloned.1.call-done = f32[16,1,24064]{2,1,0:T(1,128)} async-done(((f32[1,1,24064]{2,1,0:T(1,128)}), f32[16,1,24064]{2,1,0:T(1,128)}) %all-gather.3.cloned.1.call-update) | async-done | bytes 1540112 | tf_op jit(solution)/shard_map/all_gather | solution.py:169
  119.9 2.4 %reduce_sum.27 = f32[24064]{0:T(1024)S(1)} reduce(f32[16,1,24064]{2,1,0:T(1,128)} %all-gather.3.cloned.1.call-done, f32[]{:T(128)} %constant.1.clone.1), dimensions={0,1}, to_apply=%region_0.0 | reduce | flops 360960 | bytes 1636356 | tf_op jit(solution)/shard_map/reduce_sum | solution.py:169
  122.3 0.6 multiply_reduce_fusion
  122.9 0.7 all-reduce.2.cloned.1.call-update
  123.7 0.9 fusion.35
  124.6 20.2 %psum.15 = f32[]{:T(128)} all-reduce(f32[]{:T(128)} %multiply_reduce_fusion), channel_id=1, replica_groups=mesh['ens'=4,'lat'=8,'lon'=16] {'lat'}, use_global_device_ids=true, to_apply=%region_4.0 | all-reduce | flops 1 | bytes 8 | tf_op jit(solution)/shard_map/psum | solution.py:170
  144.8 63.0 %all-reduce.2.cloned.1.call-done = f32[24064]{0:T(1024)} async-done(((f32[24064]{0:T(1024)}), f32[24064]{0:T(1024)}) %all-reduce.2.cloned.1.call-update) | async-done | bytes 96272 | tf_op jit(solution)/shard_map/psum | solution.py:170
  207.8 1.5 multiply_reduce_fusion.1
  211.3 1.6 subtract_add_fusion
  (73 shorter events, 3.4 us)
Async XLA Ops:
  7.2 19.5 %copy-start = (f32[6,6]{1,0:T(8,128)S(1)}, f32[6,6]{1,0:T(8,128)}, u32[]{:S(2)}) copy-start(f32[6,6]{1,0:T(8,128)} %param.11) | copy-start | bytes 436
  7.2 29.4 %copy-start.4 = (bf16[128,54]{0,1:T(8,128)(2,1)S(1)}, bf16[128,54]{0,1:T(8,128)(2,1)}, u32[]{:S(2)}) copy-start(bf16[128,54]{0,1:T(8,128)(2,1)} %param.13) | copy-start | bytes 41476
  7.2 112.7 %all-gather.3.cloned.1.call-start = ((), (), s32[]{:S(2)}) async-start(), calls=%async_computation.1 | async-start | bytes 1636352 | tf_op jit(solution)/shard_map/all_gather | solution.py:169
  8.2 10.3 %collective-permute-start = (f32[6,16,1]{2,1,0:T(8,128)S(1)}, f32[6,16,1]{2,1,0:T(8,128)S(1)}, u32[]{:S(2)}, u32[]{:S(2)}) collective-permute-start(f32[6,16,1]{2,1,0:T(8,128)S(1)} %get-tuple-element.30), channel_id=1, source_target_pairs={{0,1},{1,2},{2,3},{3,4},{4,5},{5,6},{6,7},{7,8},{8,9},{9,10},{10,1... | collective-permute-start | bytes 1160 | tf_op jit(solution)/shard_map/ppermute | solution.py:20
  8.2 10.2 %collective-permute-start.1 = (f32[6,16,1]{2,1,0:T(8,128)S(1)}, f32[6,16,1]{2,1,0:T(8,128)S(1)}, u32[]{:S(2)}, u32[]{:S(2)}) collective-permute-start(f32[6,16,1]{2,1,0:T(8,128)S(1)} %get-tuple-element.31), channel_id=1, source_target_pairs={{1,0},{2,1},{3,2},{4,3},{5,4},{6,5},{7,6},{8,7},{9,8},{10,9},{11,1... | collective-permute-start | bytes 1160 | tf_op jit(solution)/shard_map/ppermute | solution.py:21
  19.3 17.7 %copy-start.3 = (bf16[128,128]{1,0:T(8,128)(2,1)S(1)}, bf16[128,128]{1,0:T(8,128)(2,1)}, u32[]{:S(2)}) copy-start(bf16[128,128]{1,0:T(8,128)(2,1)} %param.14) | copy-start | bytes 98308
  19.3 9.1 %collective-permute-start.3 = (f32[6,1,130]{2,1,0:T(1,128)S(1)}, f32[6,1,130]{2,1,0:T(1,128)S(1)}, u32[]{:S(2)}, u32[]{:S(2)}) collective-permute-start(f32[6,1,130]{2,1,0:T(1,128)S(1)} %get-tuple-element.26), channel_id=1, source_target_pairs={{16,0},{32,16},{48,32},{64,48},{80,64},{96,80},{112,96},{17,1},{33... | collective-permute-start | bytes 9368 | tf_op jit(solution)/shard_map/ppermute | solution.py:21
  24.8 7.6 %collective-permute-start.2 = (f32[6,1,130]{2,1,0:T(1,128)S(1)}, f32[6,1,130]{2,1,0:T(1,128)S(1)}, u32[]{:S(2)}, u32[]{:S(2)}) collective-permute-start(f32[6,1,130]{2,1,0:T(1,128)S(1)} %get-tuple-element.27), channel_id=1, source_target_pairs={{0,16},{16,32},{32,48},{48,64},{64,80},{80,96},{96,112},{1,17},{17... | collective-permute-start | bytes 9368 | tf_op jit(solution)/shard_map/ppermute | solution.py:20
  34.5 2.7 %copy-start.8 = (bf16[6,128]{1,0:T(8,128)(2,1)S(1)}, bf16[6,128]{1,0:T(8,128)(2,1)}, u32[]{:S(2)}) copy-start(bf16[6,128]{1,0:T(8,128)(2,1)} %param.15) | copy-start | bytes 4612
  36.5 1.0 copy-start.1
  36.5 1.0 copy-start.5
  37.8 4.7 %collective-permute-start.4 = (f32[6,16,1]{2,1,0:T(8,128)S(1)}, f32[6,16,1]{2,1,0:T(8,128)S(1)}, u32[]{:S(2)}, u32[]{:S(2)}) collective-permute-start(f32[6,16,1]{2,1,0:T(8,128)S(1)} %get-tuple-element.28), channel_id=1, source_target_pairs={{0,1},{1,2},{2,3},{3,4},{4,5},{5,6},{6,7},{7,8},{8,9},{9,10},{10,1... | collective-permute-start | bytes 1160 | tf_op jit(solution)/shard_map/ppermute | solution.py:20
  37.8 4.7 %collective-permute-start.5 = (f32[6,16,1]{2,1,0:T(8,128)S(1)}, f32[6,16,1]{2,1,0:T(8,128)S(1)}, u32[]{:S(2)}, u32[]{:S(2)}) collective-permute-start(f32[6,16,1]{2,1,0:T(8,128)S(1)} %get-tuple-element.29), channel_id=1, source_target_pairs={{1,0},{2,1},{3,2},{4,3},{5,4},{6,5},{7,6},{8,7},{9,8},{10,9},{11,1... | collective-permute-start | bytes 1160 | tf_op jit(solution)/shard_map/ppermute | solution.py:21
  42.6 6.1 %collective-permute-start.7 = (f32[6,1,130]{2,1,0:T(1,128)S(1)}, f32[6,1,130]{2,1,0:T(1,128)S(1)}, u32[]{:S(2)}, u32[]{:S(2)}) collective-permute-start(f32[6,1,130]{2,1,0:T(1,128)S(1)} %get-tuple-element.22), channel_id=1, source_target_pairs={{16,0},{32,16},{48,32},{64,48},{80,64},{96,80},{112,96},{17,1},{33... | collective-permute-start | bytes 9368 | tf_op jit(solution)/shard_map/ppermute | solution.py:21
  44.7 7.6 %collective-permute-start.6 = (f32[6,1,130]{2,1,0:T(1,128)S(1)}, f32[6,1,130]{2,1,0:T(1,128)S(1)}, u32[]{:S(2)}, u32[]{:S(2)}) collective-permute-start(f32[6,1,130]{2,1,0:T(1,128)S(1)} %get-tuple-element.23), channel_id=1, source_target_pairs={{0,16},{16,32},{32,48},{48,64},{64,80},{80,96},{96,112},{1,17},{17... | collective-permute-start | bytes 9368 | tf_op jit(solution)/shard_map/ppermute | solution.py:20
  53.1 1.0 copy-start.7
  57.9 8.9 %collective-permute-start.8 = (f32[54,16,1]{2,1,0:T(8,128)S(1)}, f32[54,16,1]{2,1,0:T(8,128)S(1)}, u32[]{:S(2)}, u32[]{:S(2)}) collective-permute-start(f32[54,16,1]{2,1,0:T(8,128)S(1)} %get-tuple-element.18), channel_id=1, source_target_pairs={{0,1},{1,2},{2,3},{3,4},{4,5},{5,6},{6,7},{7,8},{8,9},{9,10},{10,1... | collective-permute-start | bytes 10376 | tf_op jit(solution)/shard_map/ppermute | solution.py:20
  57.9 8.9 %collective-permute-start.9 = (f32[54,16,1]{2,1,0:T(8,128)S(1)}, f32[54,16,1]{2,1,0:T(8,128)S(1)}, u32[]{:S(2)}, u32[]{:S(2)}) collective-permute-start(f32[54,16,1]{2,1,0:T(8,128)S(1)} %get-tuple-element.19), channel_id=1, source_target_pairs={{1,0},{2,1},{3,2},{4,3},{5,4},{6,5},{7,6},{8,7},{9,8},{10,9},{11,1... | collective-permute-start | bytes 10376 | tf_op jit(solution)/shard_map/ppermute | solution.py:21
  67.9 6.4 %collective-permute-start.10 = (f32[54,1,130]{2,1,0:T(1,128)}, f32[54,1,130]{2,1,0:T(1,128)}, u32[]{:S(2)}, u32[]{:S(2)}) collective-permute-start(f32[54,1,130]{2,1,0:T(1,128)} %get-tuple-element.14), channel_id=1, source_target_pairs={{16,0},{32,16},{48,32},{64,48},{80,64},{96,80},{112,96},{17,1},{33... | collective-permute-start | bytes 84248 | tf_op jit(solution)/shard_map/ppermute | solution.py:21
  69.8 8.5 %collective-permute-start.11 = (f32[54,1,130]{2,1,0:T(1,128)}, f32[54,1,130]{2,1,0:T(1,128)}, u32[]{:S(2)}, u32[]{:S(2)}) collective-permute-start(f32[54,1,130]{2,1,0:T(1,128)} %get-tuple-element.15), channel_id=1, source_target_pairs={{0,16},{16,32},{32,48},{48,64},{64,80},{80,96},{96,112},{1,17},{17... | collective-permute-start | bytes 84248 | tf_op jit(solution)/shard_map/ppermute | solution.py:20
  83.7 8.9 %collective-permute-start.12 = (f32[54,16,1]{2,1,0:T(8,128)S(1)}, f32[54,16,1]{2,1,0:T(8,128)S(1)}, u32[]{:S(2)}, u32[]{:S(2)}) collective-permute-start(f32[54,16,1]{2,1,0:T(8,128)S(1)} %get-tuple-element.16), channel_id=1, source_target_pairs={{0,1},{1,2},{2,3},{3,4},{4,5},{5,6},{6,7},{7,8},{8,9},{9,10},{10,1... | collective-permute-start | bytes 10376 | tf_op jit(solution)/shard_map/ppermute | solution.py:20
  83.7 9.8 %collective-permute-start.13 = (f32[54,16,1]{2,1,0:T(8,128)S(1)}, f32[54,16,1]{2,1,0:T(8,128)S(1)}, u32[]{:S(2)}, u32[]{:S(2)}) collective-permute-start(f32[54,16,1]{2,1,0:T(8,128)S(1)} %get-tuple-element.17), channel_id=1, source_target_pairs={{1,0},{2,1},{3,2},{4,3},{5,4},{6,5},{7,6},{8,7},{9,8},{10,9},{11,1... | collective-permute-start | bytes 10376 | tf_op jit(solution)/shard_map/ppermute | solution.py:21
  93.9 29.7 %collective-permute-start.14 = (f32[54,1,130]{2,1,0:T(1,128)S(1)}, f32[54,1,130]{2,1,0:T(1,128)S(1)}, u32[]{:S(2)}, u32[]{:S(2)}) collective-permute-start(f32[54,1,130]{2,1,0:T(1,128)S(1)} %get-tuple-element.12), channel_id=1, source_target_pairs={{16,0},{32,16},{48,32},{64,48},{80,64},{96,80},{112,96},{17,1},{33... | collective-permute-start | bytes 84248 | tf_op jit(solution)/shard_map/ppermute | solution.py:21
  95.9 115.4 %copy-start.6 = (f32[24064]{0:T(1024)S(1)}, f32[24064]{0:T(1024)}, u32[]{:S(2)}) copy-start(f32[24064]{0:T(1024)} %param.17) | copy-start | bytes 288772
  95.9 27.8 %collective-permute-start.15 = (f32[54,1,130]{2,1,0:T(1,128)S(1)}, f32[54,1,130]{2,1,0:T(1,128)S(1)}, u32[]{:S(2)}, u32[]{:S(2)}) collective-permute-start(f32[54,1,130]{2,1,0:T(1,128)S(1)} %get-tuple-element.13), channel_id=1, source_target_pairs={{0,16},{16,32},{32,48},{48,64},{64,80},{80,96},{96,112},{1,17},{17... | collective-permute-start | bytes 84248 | tf_op jit(solution)/shard_map/ppermute | solution.py:20
  122.3 0.6 copy-start.2
  122.9 84.9 %all-reduce.2.cloned.1.call-start = ((), (), s32[]{:S(2)}) async-start(), calls=%async_computation | async-start | bytes 196608 | tf_op jit(solution)/shard_map/psum | solution.py:170
Sparse Core Ops, SparseCore 0:
  82.0 37.9 all-gather.2
  127.3 80.5 all-reduce.1
